TPU v7x, 1024 devices: a whole 4x4x32 slice. The times are simulated.
1024 devices in a mesh: dp: 8 (over x, core), expert: 32 (over z), head: 4 (over y).
Axes of the slice: x: 4, y: 4, z: 32, core: 2. Of those that a mesh axis runs over, the one named last changes fastest.
Arguments:
- latent: bfloat16 [10240, 1024], P(('dp', 'expert')), may hold values from -6 to 6
- cotangent: bfloat16 [10240, 1024], P(('dp', 'expert')), may hold values from -6 to 6
- routes: int32 [10240, 8], P(('dp', 'expert')), may hold values from 0 to 63, all different within a row; in each aligned block of 40 rows (0 to 39, 40 to 79, ...) at most 6 rows name the same one
- gate_values: float32 [10240, 8], P(('dp', 'expert')), may hold values from 0.05 to 0.5
- weight_in: bfloat16 [64, 2048, 1024], P('expert', 'head'), may hold values from -0.1875 to 0.1875
- weight_out: bfloat16 [64, 2048, 1024], P('expert', 'head'), may hold values from -0.125 to 0.125
Outputs:
- moe_out: bfloat16 [10240, 1024], P(('dp', 'expert'))
- latent_grad: bfloat16 [10240, 1024], P(('dp', 'expert'))
- weight_in_grad: bfloat16 [64, 2048, 1024], P('expert', 'head', 'dp')
- weight_out_grad: bfloat16 [64, 2048, 1024], P('expert', 'head', 'dp')
Inputs may be any that keep to these rules, and one draw needn't show every extreme that they name: `routes`: each row names 8 different experts. Among the rows of one device (40 rows in an aligned block), no expert is named by more than 6 rows, a bound that some block reaches.
All inputs are finite; a program needn't handle non-finite values.
Results may differ from a plain program's by a relative error of at most 0.017.
Values may be sent and summed in bfloat16 or wider, within the bound.
A program may use at most 64 MiB of HBM per device.

v0:
```python
import jax
import jax.numpy as jnp
from jax import lax
from jax.sharding import PartitionSpec as P


def route_ranks(flat_routes, expert_total):
    onehot = (flat_routes[:, None] == jnp.arange(expert_total, dtype=jnp.int32)[None, :]).astype(
        jnp.int32
    )
    before = jnp.cumsum(onehot, axis=0) - onehot
    return jnp.sum(before * onehot, axis=1)


def on_device(latent, cotangent, routes, gate_values, weight_in, weight_out):
    token_count, latent_width = latent.shape
    route_count = routes.shape[1]
    owners = lax.axis_size("expert")
    head_count = lax.axis_size("head")
    local_experts = weight_in.shape[0]
    expert_total = local_experts * owners
    capacity = 2 * max(
        1, min(token_count // 2, 3 * token_count * route_count // (4 * expert_total))
    )
    per_owner = local_experts * capacity
    slot_count = owners * per_owner
    flat_routes = routes.reshape(-1)
    target = (
        flat_routes // local_experts * per_owner
        + flat_routes % local_experts * capacity
        + route_ranks(flat_routes, expert_total)
    )
    matches = jnp.arange(slot_count, dtype=jnp.int32)[:, None] == target[None, :]
    placed = matches.reshape(slot_count, token_count, route_count)
    ones_map = jnp.any(placed, axis=2).astype(jnp.bfloat16)
    gate_map = jnp.sum(jnp.where(placed, gate_values[None, :, :], 0.0), axis=2)
    send_rows = jnp.dot(ones_map, latent, preferred_element_type=jnp.float32).astype(jnp.bfloat16)
    send_grads = jnp.dot(
        gate_map,
        cotangent.astype(jnp.float32),
        precision=lax.Precision.HIGHEST,
        preferred_element_type=jnp.float32,
    ).astype(jnp.bfloat16)
    shape_sent = (owners, local_experts, capacity, latent_width)
    got_rows, got_grads = (
        lax.all_to_all(
            send_rows.reshape(shape_sent), "expert", split_axis=0, concat_axis=0, tiled=True
        ),
        lax.all_to_all(
            send_grads.reshape(shape_sent), "expert", split_axis=0, concat_axis=0, tiled=True
        ),
    )
    pre_act = jnp.einsum("secl,ehl->sech", got_rows, weight_in, preferred_element_type=jnp.float32)
    positive = jnp.maximum(pre_act, 0.0)
    hidden_act = (positive * positive).astype(jnp.bfloat16)
    out_part = jnp.einsum(
        "sech,ehl->secl", hidden_act, weight_out, preferred_element_type=jnp.float32
    )
    grad_act = jnp.einsum(
        "secl,ehl->sech", got_grads, weight_out, preferred_element_type=jnp.float32
    )
    grad_pre = (grad_act * 2.0 * positive).astype(jnp.bfloat16)
    back_part = jnp.einsum(
        "sech,ehl->secl", grad_pre, weight_in, preferred_element_type=jnp.float32
    )
    in_partial = jnp.einsum(
        "sech,secl->ehl", grad_pre, got_rows, preferred_element_type=jnp.float32
    )
    out_partial = jnp.einsum(
        "sech,secl->ehl", hidden_act, got_grads, preferred_element_type=jnp.float32
    )
    summed_in, summed_out = (
        lax.psum_scatter(
            in_partial.astype(jnp.bfloat16), "dp", scatter_dimension=2, tiled=True
        ).astype(jnp.float32),
        lax.psum_scatter(
            out_partial.astype(jnp.bfloat16), "dp", scatter_dimension=2, tiled=True
        ).astype(jnp.float32),
    )
    weight_in_grad = summed_in.astype(jnp.bfloat16)
    weight_out_grad = summed_out.astype(jnp.bfloat16)
    flat_gates = gate_values.reshape(-1)
    share_width = per_owner // head_count
    owned_shape = (owners, per_owner, latent_width)
    share_out, share_back = (
        lax.psum_scatter(
            out_part.reshape(owned_shape).astype(jnp.bfloat16),
            "head",
            scatter_dimension=1,
            tiled=True,
        ).astype(jnp.float32),
        lax.psum_scatter(
            back_part.reshape(owned_shape).astype(jnp.bfloat16),
            "head",
            scatter_dimension=1,
            tiled=True,
        ).astype(jnp.float32),
    )
    back_out, back_grad = (
        lax.all_to_all(
            share_out.astype(jnp.bfloat16), "expert", split_axis=0, concat_axis=0, tiled=True
        ).astype(share_out.dtype),
        lax.all_to_all(
            share_back.astype(jnp.bfloat16), "expert", split_axis=0, concat_axis=0, tiled=True
        ).astype(share_back.dtype),
    )
    within = target % per_owner
    mine = within // share_width == lax.axis_index("head")
    picked = target // per_owner * share_width + within % share_width
    out_rows = jnp.take(back_out.reshape(-1, latent_width), picked, axis=0)
    grad_rows = jnp.take(back_grad.reshape(-1, latent_width), picked, axis=0)
    out_weight = jnp.where(mine, flat_gates, 0.0)
    grad_weight = jnp.where(mine, 1.0, 0.0)
    out_total = jnp.sum(
        (out_weight[:, None] * out_rows).reshape(token_count, route_count, latent_width), axis=1
    )
    grad_total = jnp.sum(
        (grad_weight[:, None] * grad_rows).reshape(token_count, route_count, latent_width), axis=1
    )
    moe_out, latent_grad = (
        lax.psum(out_total.astype(jnp.bfloat16), "head").astype(jnp.float32),
        lax.psum(grad_total.astype(jnp.bfloat16), "head").astype(jnp.float32),
    )
    return (
        moe_out.astype(jnp.bfloat16),
        latent_grad.astype(jnp.bfloat16),
        weight_in_grad,
        weight_out_grad,
    )


def solution(mesh):
    in_specs = (
        P(("dp", "expert"), None),
        P(("dp", "expert"), None),
        P(("dp", "expert"), None),
        P(("dp", "expert"), None),
        P("expert", "head", None),
        P("expert", "head", None),
    )
    out_specs = (
        P(("dp", "expert"), None),
        P(("dp", "expert"), None),
        P("expert", "head", "dp"),
        P("expert", "head", "dp"),
    )
    return jax.shard_map(
        on_device, mesh=mesh, in_specs=in_specs, out_specs=out_specs, check_vma=False
    )
```

profile of v0, /device:TPU:6, one launch (start us, length us, event | category | flops | bytes accessed | tf_op | source)
XLA Modules:
  0.0 489.9 jit_solution(16343677906867707786)
XLA Ops:
  9.9 2.2 convolution_convert_fusion.1
  15.1 28.8 %all-to-all-start = ((bf16[32,2,6,1024]{3,1,2,0:T(2,128)(2,1)}), bf16[32,2,6,1024]{3,1,2,0:T(2,128)(2,1)}, u32[]{:S(2)}, u32[]{:S(2)}) async-start(bf16[32,2,6,1024]{3,1,2,0:T(2,128)(2,1)} %copy.69), calls=%async_computation | async-start | bytes 1572864 | tf_op jit(solution)/shard_map/all_to_all | solution.py:46
  49.1 81.8 %all-to-all-done = bf16[32,2,6,1024]{3,1,2,0:T(2,128)(2,1)} async-done(((bf16[32,2,6,1024]{3,1,2,0:T(2,128)(2,1)}), bf16[32,2,6,1024]{3,1,2,0:T(2,128)(2,1)}, u32[]{:S(2)}, u32[]{:S(2)}) %all-to-all-start) | async-done | bytes 786464 | tf_op jit(solution)/shard_map/all_to_all | solution.py:46
  130.9 4.6 all-to-all-start.2
  135.6 2.0 fusion.17
  137.6 84.8 %all-to-all-done.2 = bf16[32,2,6,1024]{3,1,2,0:T(2,128)(2,1)} async-done(((bf16[32,2,6,1024]{3,1,2,0:T(2,128)(2,1)}), bf16[32,2,6,1024]{3,1,2,0:T(2,128)(2,1)}, u32[]{:S(2)}, u32[]{:S(2)}) %all-to-all-start.2) | async-done | bytes 786464 | tf_op jit(solution)/shard_map/all_to_all | solution.py:49
  222.4 2.8 fusion.26
  226.8 3.1 fusion.8
  229.9 3.3 bitcast_convert_fusion.1
  233.2 6.2 %copy.82 = bf16[2,512,1024]{1,0,2:T(2,128)(2,1)} copy(bf16[2,512,1024]{2,1,0:T(8,128)(2,1)} %bitcast_convert_fusion.1) | data formatting | bytes 4194304
  239.4 3.5 copy.88
  243.0 3.3 bitcast_convert_fusion
  246.3 6.1 %copy.84 = bf16[2,512,1024]{1,0,2:T(2,128)(2,1)} copy(bf16[2,512,1024]{2,1,0:T(8,128)(2,1)} %bitcast_convert_fusion) | data formatting | bytes 4194304
  252.4 3.5 copy.89
  257.7 15.2 %all-to-all-start.3 = ((bf16[32,3,1024]{2,1,0:T(4,128)(2,1)}), bf16[32,3,1024]{2,1,0:T(4,128)(2,1)S(1)}, u32[]{:S(2)}, u32[]{:S(2)}) async-start(bf16[32,3,1024]{2,1,0:T(4,128)(2,1)} %copy.75), calls=%async_computation.5 | async-start | bytes 524288 | tf_op jit(solution)/shard_map/all_to_all | solution.py:103
  273.0 18.9 %reduce-scatter.9.cloned.1.call-done = bf16[32,3,1024]{2,0,1:T(8,128)(2,1)} async-done(((bf16[32,12,1024]{2,0,1:T(8,128)(2,1)}), bf16[32,3,1024]{2,0,1:T(8,128)(2,1)}) %reduce-scatter.9.cloned.1.call-update) | async-done | bytes 196624 | tf_op jit(solution)/shard_map/reduce_scatter | solution.py:86
  293.7 20.8 %all-to-all-done.3 = bf16[32,3,1024]{2,1,0:T(4,128)(2,1)S(1)} async-done(((bf16[32,3,1024]{2,1,0:T(4,128)(2,1)}), bf16[32,3,1024]{2,1,0:T(4,128)(2,1)S(1)}, u32[]{:S(2)}, u32[]{:S(2)}) %all-to-all-start.3) | async-done | bytes 196640 | tf_op jit(solution)/shard_map/all_to_all | solution.py:103
  314.5 4.1 all-to-all-start.1
  319.0 2.4 gather_fusion.1
  321.4 37.5 %all-to-all-done.1 = bf16[32,3,1024]{2,1,0:T(4,128)(2,1)S(1)} async-done(((bf16[32,3,1024]{2,1,0:T(4,128)(2,1)}), bf16[32,3,1024]{2,1,0:T(4,128)(2,1)S(1)}, u32[]{:S(2)}, u32[]{:S(2)}) %all-to-all-start.1) | async-done | bytes 196640 | tf_op jit(solution)/shard_map/all_to_all | solution.py:100
  359.1 2.4 gather_fusion
  361.4 3.3 bitcast_reduce_fusion
  366.8 31.0 %reduce-scatter.15.cloned.1.call-done = bf16[128,1024]{1,0:T(8,128)(2,1)} async-done(((bf16[1024,1024]{1,0:T(8,128)(2,1)}), bf16[128,1024]{1,0:T(8,128)(2,1)}) %reduce-scatter.15.cloned.1.call-update) | async-done | bytes 262160
  399.9 80.4 %all-reduce.4.cloned.1.call-done = (bf16[40,1024]{1,0:T(8,128)(2,1)}, bf16[40,1024]{1,0:T(8,128)(2,1)}) async-done(((bf16[40,1024]{1,0:T(8,128)(2,1)}, bf16[40,1024]{1,0:T(8,128)(2,1)}), (bf16[40,1024]{1,0:T(8,128)(2,1)}, bf16[40,1024]{1,0:T(8,128)(2,1)})) %all-reduce.4.cloned.1.call-update) | async-done | bytes 163856 | tf_op jit(solution)/shard_map/psum | solution.py:121
  (53 shorter events, 23.8 us)
Async XLA Ops:
  7.2 128.4 %copy-start = (bf16[2,512,1024]{2,1,0:T(8,128)(2,1)S(1)}, bf16[2,512,1024]{2,1,0:T(8,128)(2,1)}, u32[]{:S(2)}) copy-start(bf16[2,512,1024]{2,1,0:T(8,128)(2,1)} %param.12) | copy-start | bytes 6291460
  13.4 30.6 %copy-start.2 = (f32[40,8]{0,1:T(8,128)S(1)}, f32[40,8]{0,1:T(8,128)}, u32[]{:S(2)}) copy-start(f32[40,8]{0,1:T(8,128)} %param.11) | copy-start | bytes 3844
  13.4 30.9 %copy-start.1 = (bf16[40,1024]{1,0:T(8,128)(2,1)S(1)}, bf16[40,1024]{1,0:T(8,128)(2,1)}, u32[]{:S(2)}) copy-start(bf16[40,1024]{1,0:T(8,128)(2,1)} %param.9) | copy-start | bytes 245764
  15.1 115.7 %all-to-all-start = ((bf16[32,2,6,1024]{3,1,2,0:T(2,128)(2,1)}), bf16[32,2,6,1024]{3,1,2,0:T(2,128)(2,1)}, u32[]{:S(2)}, u32[]{:S(2)}) async-start(bf16[32,2,6,1024]{3,1,2,0:T(2,128)(2,1)} %copy.69), calls=%async_computation | async-start | bytes 1572864 | tf_op jit(solution)/shard_map/all_to_all | solution.py:46
  130.9 91.6 %all-to-all-start.2 = ((bf16[32,2,6,1024]{3,1,2,0:T(2,128)(2,1)}), bf16[32,2,6,1024]{3,1,2,0:T(2,128)(2,1)}, u32[]{:S(2)}, u32[]{:S(2)}) async-start(bf16[32,2,6,1024]{3,1,2,0:T(2,128)(2,1)} %copy.73), calls=%async_computation.3 | async-start | bytes 1572864 | tf_op jit(solution)/shard_map/all_to_all | solution.py:49
  135.5 120.4 %reduce-scatter.11.cloned.1.call-start = ((), (), s32[]{:S(2)}) async-start(), calls=%async_computation.9 | async-start | bytes 983040 | tf_op jit(solution)/shard_map/reduce_scatter | solution.py:92
  226.7 65.2 %reduce-scatter.9.cloned.1.call-start = ((), (), s32[]{:S(2)}) async-start(), calls=%async_computation.8 | async-start | bytes 983040 | tf_op jit(solution)/shard_map/reduce_scatter | solution.py:86
  229.8 134.9 %reduce-scatter.13.cloned.1.call-start = ((), (), s32[]{:S(2)}) async-start(), calls=%async_computation.10 | async-start | bytes 2359296
  242.9 154.9 %reduce-scatter.15.cloned.1.call-start = ((), (), s32[]{:S(2)}) async-start(), calls=%async_computation.11 | async-start | bytes 2359296
  257.7 56.8 %all-to-all-start.3 = ((bf16[32,3,1024]{2,1,0:T(4,128)(2,1)}), bf16[32,3,1024]{2,1,0:T(4,128)(2,1)S(1)}, u32[]{:S(2)}, u32[]{:S(2)}) async-start(bf16[32,3,1024]{2,1,0:T(4,128)(2,1)} %copy.75), calls=%async_computation.5 | async-start | bytes 524288 | tf_op jit(solution)/shard_map/all_to_all | solution.py:103
  314.5 44.4 %all-to-all-start.1 = ((bf16[32,3,1024]{2,1,0:T(4,128)(2,1)}), bf16[32,3,1024]{2,1,0:T(4,128)(2,1)S(1)}, u32[]{:S(2)}, u32[]{:S(2)}) async-start(bf16[32,3,1024]{2,1,0:T(4,128)(2,1)} %copy.71), calls=%async_computation.2 | async-start | bytes 524288 | tf_op jit(solution)/shard_map/all_to_all | solution.py:100
  318.6 161.7 %all-reduce.4.cloned.1.call-start = ((), (), s32[]{:S(2)}) async-start(), calls=%async_computation.12 | async-start | bytes 327680 | tf_op jit(solution)/shard_map/psum | solution.py:121
Sparse Core Ops, SparseCore 0:
  226.8 21.3 reduce-scatter.10
  251.6 40.2 reduce-scatter.8
  295.3 48.8 reduce-scatter.12
  347.5 50.2 reduce-scatter.14
  400.6 79.7 all-reduce.3
where the time goes:
time: 492 us; the launch traced here: 490 us
  waiting for transfers between devices  355 us (72%)
  starting transfers between devices  53 us (11%)
  local copies, waits for them, and re-layouts  42.7 us (9%)
  matrix products  19.8 us (4%)
  between operations  14 us (3%)
  other arithmetic  4.92 us (1%)
    all_to_all x1, waiting for transfers between devices, on_device(): lax.all_to_all(send_grads.reshape(shape_sent), 'expert', split_axis=0, co...  84.8 us
    all_to_all x1, waiting for transfers between devices, on_device(): lax.all_to_all(send_rows.reshape(shape_sent), 'expert', split_axis=0, con...  81.8 us
    psum x1, waiting for transfers between devices, on_device(): lax.psum(out_total.astype(jnp.bfloat16), 'head').astype(jnp.float32)  80.4 us
    all_to_all x1, waiting for transfers between devices, on_device(): lax.all_to_all(share_out.astype(jnp.bfloat16), 'expert', split_axis=0, co...  37.5 us
    unnamed x7, waiting for transfers between devices  31.1 us
    all_to_all x1, starting transfers between devices, on_device(): lax.all_to_all(send_rows.reshape(shape_sent), 'expert', split_axis=0, con...  28.8 us
    unnamed x18, local copies, waits for them, and re-layouts  27.5 us
    all_to_all x1, waiting for transfers between devices, on_device(): lax.all_to_all(share_back.astype(jnp.bfloat16), 'expert', split_axis=0, c...  20.8 us
  transfers between devices with their start and end apart: 9, of which 7 were waited for; matrix products, arithmetic and copies ran while one was open for 11% of the time, Pallas kernels for 0%

commit v1 on v0

v1 whole, which is shorter than its diff:
```python
import jax
import jax.numpy as jnp
from jax import lax
from jax.sharding import PartitionSpec as P

CAPACITY = 6


def on_device(latent, cotangent, routes, gate_values, weight_in, weight_out):
    token_count, latent_width = latent.shape
    route_count = routes.shape[1]
    owners = lax.axis_size("expert")
    heads = lax.axis_size("head")
    local = weight_in.shape[0]
    quarter = latent_width // heads
    me = lax.axis_index("expert")
    head = lax.axis_index("head")
    slots = local * CAPACITY
    f32, bf16 = jnp.float32, jnp.bfloat16

    own = lax.dynamic_slice(
        jnp.concatenate([latent, cotangent], 0), (0, head * quarter), (2 * token_count, quarter)
    )
    meta = jnp.concatenate([routes.astype(f32), gate_values], axis=1)
    meta = lax.all_gather(meta, "expert", axis=0)
    data = lax.all_gather(own, "expert", axis=0)

    expert = (me * local + jnp.arange(local)).astype(f32)
    hit = meta[:, :, None, :route_count] == expert[None, None, :, None]
    chosen = jnp.any(hit, axis=3)
    gates = jnp.sum(jnp.where(hit, meta[:, :, None, route_count:], 0.0), axis=3)
    count = chosen.astype(jnp.int32)
    rank = jnp.cumsum(count, axis=1) - count
    place = (rank[..., None] == jnp.arange(CAPACITY)) & chosen[..., None]
    gate_slot = jnp.sum(jnp.where(place, gates[..., None], 0.0), axis=1)
    gate_slot = gate_slot.reshape(owners, slots, 1)
    place = place.astype(bf16).reshape(owners, token_count, slots)

    rows = jnp.einsum("stc,stl->scl", place, data[:, :token_count], preferred_element_type=f32)
    grads = jnp.einsum("stc,stl->scl", place, data[:, token_count:], preferred_element_type=f32)
    both = jnp.stack([rows.astype(bf16), (grads * gate_slot).astype(bf16)])
    both = lax.all_gather(both, "head", axis=3, tiled=True)
    both = both.reshape(2, owners, local, CAPACITY, latent_width)
    got = both.transpose(0, 2, 1, 3, 4).reshape(2, local, owners * CAPACITY, latent_width)
    got_rows, got_grads = got[0], got[1]

    pre_act = jnp.einsum("ecl,ehl->ech", got_rows, weight_in, preferred_element_type=f32)
    positive = jnp.maximum(pre_act, 0.0)
    hidden_act = (positive * positive).astype(bf16)
    out_part = jnp.einsum("ech,ehl->ecl", hidden_act, weight_out, preferred_element_type=f32)
    grad_act = jnp.einsum("ecl,ehl->ech", got_grads, weight_out, preferred_element_type=f32)
    grad_pre = (grad_act * 2.0 * positive).astype(bf16)
    back_part = jnp.einsum("ech,ehl->ecl", grad_pre, weight_in, preferred_element_type=f32)
    parts = jnp.stack([out_part.astype(bf16), back_part.astype(bf16)])
    share = lax.psum_scatter(parts, "head", scatter_dimension=3, tiled=True)
    in_partial = jnp.einsum("ech,ecl->ehl", grad_pre, got_rows, preferred_element_type=f32)
    out_partial = jnp.einsum("ech,ecl->ehl", hidden_act, got_grads, preferred_element_type=f32)
    partial = jnp.stack([in_partial.astype(bf16), out_partial.astype(bf16)])
    summed = lax.psum_scatter(partial, "dp", scatter_dimension=3, tiled=True)

    share = share.reshape(2, local, owners, CAPACITY, quarter).transpose(0, 2, 1, 3, 4)
    share = share.reshape(2, owners, slots, quarter)
    scaled = (share[0].astype(f32) * gate_slot).astype(bf16)
    out_tok = jnp.einsum("stc,scl->stl", place, scaled, preferred_element_type=f32)
    back_tok = jnp.einsum("stc,scl->stl", place, share[1], preferred_element_type=f32)
    tokens = jnp.stack([out_tok.astype(bf16), back_tok.astype(bf16)], axis=1)
    mine = lax.psum_scatter(tokens, "expert", scatter_dimension=0)
    full = lax.all_gather(mine, "head", axis=2, tiled=True)
    return full[0], full[1], summed[0], summed[1]


def solution(mesh):
    in_specs = (
        P(("dp", "expert"), None),
        P(("dp", "expert"), None),
        P(("dp", "expert"), None),
        P(("dp", "expert"), None),
        P("expert", "head", None),
        P("expert", "head", None),
    )
    out_specs = (
        P(("dp", "expert"), None),
        P(("dp", "expert"), None),
        P("expert", "head", "dp"),
        P("expert", "head", "dp"),
    )
    return jax.shard_map(
        on_device, mesh=mesh, in_specs=in_specs, out_specs=out_specs, check_vma=False
    )
```

time: 492 us -> 591 us (1.20)
  blocking collectives: 0 us -> 81.8 us
  waiting for transfers between devices: 355 us -> 436 us
  starting transfers between devices: 53 us -> 0.21 us
  matrix products: 19.8 us -> 9.3 us
  local copies, waits for them, and re-layouts: 42.7 us -> 32.9 us
  other arithmetic: 4.92 us -> 12.1 us
    unnamed x7, waiting for transfers between devices: 31.1 us -> 275 us
    all_to_all x4 -> x0, waiting for transfers between devices: 225 us -> none  [the longest x1 84.8 us: on_device(): lax.all_to_all(send_grads.reshape(shape_sent), 'expert', split_axis=0, co...]
    all_gather x0 -> x2, waiting for transfers between devices: none -> 115 us  [the longest x1 71.9 us: on_device(): data = lax.all_gather(own, 'expert', axis=0)]
    all_gather x0 -> x2, blocking collectives: none -> 81.8 us  [the longest x1 69.4 us: on_device(): meta = lax.all_gather(meta, 'expert', axis=0)]
    psum x1 -> x0, waiting for transfers between devices: 80.4 us -> none  [on_device(): lax.psum(out_total.astype(jnp.bfloat16), 'head').astype(jnp.float32)]
    all_to_all x4 -> x0, starting transfers between devices: 52.8 us -> none  [the longest x1 28.8 us: on_device(): lax.all_to_all(send_rows.reshape(shape_sent), 'expert', split_axis=0, con...]
    reduce_scatter x2 -> x1, waiting for transfers between devices: 18.9 us -> 44.9 us  [on_device(): share = lax.psum_scatter(parts, 'head', scatter_dimension=3, tiled=True)]
    dot_general x8 -> x10, matrix products: 19.8 us -> 9.3 us  [the longest x1 1.98 us: on_device(): jnp.einsum('ech,ecl->ehl', grad_pre, got_rows, preferred_element_type=f32)]
  transfers between devices with their start and end apart: 9 -> 5, of which waited for: 7 -> 5; matrix products, arithmetic and copies ran while one was open for 11% -> 6% of each run, Pallas kernels for 0% -> 0%
where the time goes in v1:
time: 591 us; the launch traced here: 586 us
  waiting for transfers between devices  436 us (74%)
  blocking collectives  81.8 us (14%)
  local copies, waits for them, and re-layouts  32.9 us (6%)
  between operations  14.1 us (2%)
  other arithmetic  12.1 us (2%)
  matrix products  9.3 us (2%)
    unnamed x7, waiting for transfers between devices  275 us
    all_gather x1, waiting for transfers between devices, on_device(): data = lax.all_gather(own, 'expert', axis=0)  71.9 us
    all_gather x1, blocking collectives, on_device(): meta = lax.all_gather(meta, 'expert', axis=0)  69.4 us
    reduce_scatter x1, waiting for transfers between devices, on_device(): share = lax.psum_scatter(parts, 'head', scatter_dimension=3, tiled=True)  44.9 us
    all_gather x1, waiting for transfers between devices, on_device(): both = lax.all_gather(both, 'head', axis=3, tiled=True)  43.5 us
    unnamed x17, local copies, waits for them, and re-layouts  24.9 us
    all_gather x1, blocking collectives, on_device(): full = lax.all_gather(mine, 'head', axis=2, tiled=True)  12.4 us
  transfers between devices with their start and end apart: 5, of which 5 were waited for; matrix products, arithmetic and copies ran while one was open for 6% of the time, Pallas kernels for 0%

profile of v1, /device:TPU:6, one launch (start us, length us, event | category | flops | bytes accessed | tf_op | source)
XLA Modules:
  0.0 585.9 jit_solution(9776944610857689477)
XLA Ops:
  7.2 1.5 fusion.26
  10.3 69.4 %all-gather.3 = f32[32,40,16]{1,2,0:T(8,128)S(1)} all-gather(f32[1,40,16]{1,2,0:T(8,128)S(1)} %maximum_bitcast_fusion), channel_id=2, replica_groups=mesh['dp'=8,'expert'=32,'head'=4] {'expert'}, dimensions={0}, use_global_device_ids=true | all-gather | bytes 84480 | tf_op jit(solution)/shard_map/all_gather | solution.py:25
  80.7 2.9 fusion.32
  84.4 71.9 %all-gather.9.cloned.1.call-done = bf16[2560,256]{1,0:T(8,128)(2,1)} async-done(((bf16[80,256]{1,0:T(8,128)(2,1)}), bf16[2560,256]{1,0:T(8,128)(2,1)}) %all-gather.9.cloned.1.call-update) | async-done | bytes 1310736 | tf_op jit(solution)/shard_map/all_gather | solution.py:26
  156.3 1.3 fusion.7
  157.7 1.3 fusion.8
  159.9 43.5 %all-gather.7.cloned.1.call-done = bf16[2,32,12,1024]{3,2,1,0:T(8,128)(2,1)} async-done(((bf16[2,32,12,256]{3,2,1,0:T(8,128)(2,1)}), bf16[2,32,12,1024]{3,2,1,0:T(8,128)(2,1)}) %all-gather.7.cloned.1.call-update) | async-done | bytes 1572880 | tf_op jit(solution)/shard_map/all_gather | solution.py:42
  203.4 2.5 copy.89
  210.7 1.3 pad_maximum_fusion.1
  212.1 44.9 %reduce-scatter.6.cloned.1.call-done = bf16[2,2,192,256]{3,2,1,0:T(8,128)(2,1)} async-done(((bf16[2,2,192,1024]{3,2,1,0:T(8,128)(2,1)}), bf16[2,2,192,256]{3,2,1,0:T(8,128)(2,1)}) %reduce-scatter.6.cloned.1.call-update) | async-done | bytes 393232 | tf_op jit(solution)/shard_map/reduce_scatter | solution.py:55
  257.0 1.4 copy.94
  259.5 1.2 pad_maximum_fusion.2
  260.8 2.0 convert_bitcast_fusion.1
  263.6 2.3 pad_maximum_fusion
  265.9 11.2 %copy.104 = bf16[2,2,512,1024]{2,1,0,3:T(2,128)(2,1)} copy(bf16[2,2,512,1024]{3,2,1,0:T(8,128)(2,1)} %pad_maximum_fusion) | data formatting | bytes 8388608
  277.0 7.8 %reshape.68 = bf16[1024,2048]{1,0:T(8,128)(2,1)} reshape(bf16[1024,2,2,512]{3,2,1,0:T(2,128)(2,1)} %bitcast.58) | data formatting | bytes 8388608
  284.8 1.3 dynamic-slice
  286.1 242.0 %all-reduce.3.cloned.1.call-done = bf16[32,2,40,256]{3,2,0,1:T(8,128)(2,1)} async-done(((bf16[32,2,40,256]{3,2,0,1:T(8,128)(2,1)}), bf16[32,2,40,256]{3,2,0,1:T(8,128)(2,1)}) %all-reduce.3.cloned.1.call-update) | async-done | bytes 1310736
  528.1 1.4 constant_dynamic-slice_fusion
  529.5 12.4 %all-gather.2 = bf16[1,2,40,1024]{3,2,0,1:T(8,128)(2,1)S(1)} all-gather(bf16[1,2,40,256]{3,2,0,1:T(8,128)(2,1)S(1)} %constant_dynamic-slice_fusion), channel_id=4, replica_groups=mesh['dp'=8,'expert'=32,'head'=4] {'head'}, dimensions={3}, use_global_device_ids=true | all-gather | bytes 204800 | tf_op jit(solution)/shard_map/all_gather | solution.py:68
  542.6 33.2 %reduce-scatter.8.cloned.1.call-done = bf16[128,2048]{1,0:T(8,128)(2,1)} async-done(((bf16[1024,2048]{1,0:T(8,128)(2,1)}), bf16[128,2048]{1,0:T(8,128)(2,1)}) %reduce-scatter.8.cloned.1.call-update) | async-done | bytes 524304
  575.8 1.4 reshape.69
  577.6 0.9 copy.107
  578.5 0.9 copy.106
  (53 shorter events, 12.0 us)
Async XLA Ops:
  7.2 201.5 %copy-start = (bf16[2,512,1024]{2,1,0:T(8,128)(2,1)S(1)}, bf16[2,512,1024]{2,1,0:T(8,128)(2,1)}, u32[]{:S(2)}) copy-start(bf16[2,512,1024]{2,1,0:T(8,128)(2,1)} %param.11) | copy-start | bytes 6291460
  7.2 149.1 %all-gather.9.cloned.1.call-start = ((), (), s32[]{:S(2)}) async-start(), calls=%async_computation.4 | async-start | bytes 1351680 | tf_op jit(solution)/shard_map/all_gather | solution.py:26
  8.8 194.7 %all-gather.7.cloned.1.call-start = ((), (), s32[]{:S(2)}) async-start(), calls=%async_computation.2 | async-start | bytes 2621440 | tf_op jit(solution)/shard_map/all_gather | solution.py:42
  159.9 97.1 %reduce-scatter.6.cloned.1.call-start = ((), (), s32[]{:S(2)}) async-start(), calls=%async_computation.3 | async-start | bytes 1966080 | tf_op jit(solution)/shard_map/reduce_scatter | solution.py:55
  206.1 1.7 copy-start.1
  206.9 2.3 copy-start.3
  207.7 1.5 copy-start.2
  212.0 316.1 %all-reduce.3.cloned.1.call-start = ((), (), s32[]{:S(2)}) async-start(), calls=%async_computation.6 | async-start | bytes 2621440
  260.7 315.0 %reduce-scatter.8.cloned.1.call-start = ((), (), s32[]{:S(2)}) async-start(), calls=%async_computation.5 | async-start | bytes 4718592
  260.8 2.0 copy-start.4
Sparse Core Ops, SparseCore 0:
  11.3 145.0 all-gather.8
  160.0 43.3 all-gather.6
  212.2 44.7 reduce-scatter.5
  260.8 267.2 all-reduce.2
  531.7 43.9 reduce-scatter.7

commit v2 on v1

v2 whole, which is shorter than its diff:
```python
import functools

import jax
import jax.numpy as jnp
from jax import lax
from jax.experimental import pallas as pl
from jax.experimental.pallas import tpu as pltpu
from jax.sharding import PartitionSpec as P

CAPACITY = 6
GROUP = 8
MESH = pl.DeviceIdType.MESH
f32, bf16 = jnp.float32, jnp.bfloat16


def nt_dot(a, b):
    return lax.dot_general(a, b, (((1,), (1,)), ((), ())), preferred_element_type=f32)


def nn_dot(a, b):
    return lax.dot_general(a, b, (((1,), (0,)), ((), ())), preferred_element_type=f32)


def tn_dot(a, b):
    return lax.dot_general(a, b, (((0,), (0,)), ((), ())), preferred_element_type=f32)


def kernel(
    dims, blk_ref, win_hbm, wout_hbm, tok_ref, wgrad_ref,
    ring, picks, gates, xrows, win, wout, acts, yown, yland, contrib, from_left, from_right,
    parts, pair, cross,
    w_sem, zs, zr, ys, yr, os_, or_, rs, rr, ps, pr, cs, cr, ts, tr,
):
    owners, heads, xs, tokens, local = dims
    half = owners // 2
    chunks = owners // GROUP
    rows = GROUP * CAPACITY
    both = 2 * tokens
    width = ring.shape[2]
    hidden = win.shape[1]
    pieces = hidden // 256

    me = lax.axis_index("expert")
    head = lax.axis_index("head")
    dp = lax.axis_index("dp")
    px, core = dp // 2, dp % 2
    right, left = lax.rem(me + 1, owners), lax.rem(me + owners - 1, owners)
    to_right, to_left = {"expert": right}, {"expert": left}
    head_at = [lax.rem(head + d, heads) for d in range(heads)]
    x_at = [lax.rem(px + d, xs) for d in range(xs)]
    sibling = {"dp": px * 2 + 1 - core}

    def remote(src, dst, send, recv, device):
        return pltpu.make_async_remote_copy(
            src_ref=src, dst_ref=dst, send_sem=send, recv_sem=recv,
            device_id=device, device_id_type=MESH,
        )

    load_in = pltpu.make_async_copy(win_hbm, win, w_sem.at[0])
    load_out = pltpu.make_async_copy(wout_hbm, wout, w_sem.at[1])
    load_in.start()
    load_out.start()
    ring[0] = blk_ref[...]

    barrier = pltpu.get_barrier_semaphore()
    partners = [to_right, to_left, sibling]
    partners += [{"head": head_at[d]} for d in range(1, heads)]
    partners += [{"dp": x_at[d] * 2 + core} for d in range(1, xs)]
    for device in partners:
        pl.semaphore_signal(barrier, inc=1, device_id=device, device_id_type=MESH)
    pl.semaphore_wait(barrier, len(partners))

    def slot_right(i):
        return jnp.maximum(2 * i - 1, 0)

    def ring_right(i):
        return remote(
            ring.at[slot_right(i - 1)], ring.at[slot_right(i)], zs.at[0, i], zr.at[0, i], to_right
        )

    def ring_left(i):
        return remote(ring.at[2 * (i - 1)], ring.at[2 * i], zs.at[1, i], zr.at[1, i], to_left)

    def spread(d, c):
        return remote(
            xrows.at[head, c], xrows.at[head, c], ys.at[d - 1, c], yr.at[d - 1, c],
            {"head": head_at[d]},
        )

    ring_right(1).start()
    ring_left(1).start()

    lane = lax.broadcasted_iota(jnp.int32, (128, 128), 1)
    depth = lax.broadcasted_iota(jnp.int32, (128, 128), 0)
    earlier = (depth < lane) & ((depth < tokens) == (lane < tokens))
    earlier = jnp.where(earlier, 1.0, 0.0).astype(bf16)
    row_id = lax.broadcasted_iota(jnp.int32, (rows, 128), 0).astype(f32)
    group_row = lax.broadcasted_iota(jnp.int32, (GROUP, 128), 0).astype(f32) * CAPACITY
    group_lane = lax.broadcasted_iota(jnp.int32, (GROUP, 128), 1)

    def select(c):
        meta = ring[pl.ds(c * GROUP, GROUP), both:both + 16, :].astype(f32)
        routes = meta[:, :8, :128]
        gate = meta[:, 8:, :128] + meta[:, :8, 128:] + meta[:, 8:, 128:]
        codes, weights = [], []
        for e in range(local):
            hit = routes == (me * local + e).astype(f32)
            chosen = jnp.max(jnp.where(hit, 1.0, 0.0), axis=1)
            weights.append(jnp.sum(jnp.where(hit, gate, 0.0), axis=1))
            rank = nn_dot(chosen.astype(bf16), earlier)
            codes.append(jnp.where(chosen > 0.5, rank + group_row, -1.0))
        by_kind = [jnp.where(group_lane < tokens, code, -1.0) for code in codes]
        by_kind += [jnp.where(group_lane >= tokens, code, -1.0) for code in codes]
        total = jnp.zeros((2 * local * rows, width), f32)
        scale = [jnp.zeros((rows, 128), f32) for _ in range(local)]
        for q in range(GROUP):
            match = [row_id == code[q:q + 1, :] for code in by_kind]
            pick = jnp.concatenate([jnp.where(m, 1.0, 0.0) for m in match], axis=0).astype(bf16)
            picks[c * GROUP + q] = pick
            block = ring[c * GROUP + q]
            total = total + nn_dot(pick[:, :both + 16], block)
            for e in range(local):
                scale[e] = scale[e] + jnp.where(match[local + e], weights[e][q:q + 1, :], 0.0)
        scale = jnp.sum(jnp.concatenate(scale, axis=0), axis=1, keepdims=True)
        gates[c] = jnp.broadcast_to(scale, (local * rows, 128))
        xrows[head, c, 0] = total[: local * rows].astype(bf16).reshape(local, rows, width)
        xrows[head, c, 1] = (total[local * rows:] * scale).astype(bf16).reshape(local, rows, width)

    def gather_group(c, carry):
        for k in range(4):
            i = c * 4 + 1 + k
            ring_right(i).wait_recv()

            @pl.when(i < half)
            def _():
                ring_right(i + 1).start()
                ring_left(i).wait_recv()

            @pl.when(i < half - 1)
            def _():
                ring_left(i + 1).start()

        select(c)
        for d in range(1, heads):
            spread(d, c).start()
        return carry

    lax.fori_loop(0, chunks, gather_group, 0)
    load_in.wait()
    load_out.wait()

    def spread_wait(c, carry):
        for d in range(1, heads):
            spread(d, c).wait()
        return carry

    lax.fori_loop(0, chunks, spread_wait, 0)

    def taken(kind, e, h):
        return xrows[h, :, kind, e].reshape(chunks * rows, width)

    def expert(e, carry):
        got = [jnp.concatenate([taken(k, e, h) for h in range(heads)], axis=1) for k in range(2)]
        for p in range(pieces):
            part = pl.ds(p * 256, 256)
            positive = jnp.maximum(nt_dot(got[0], win[e, part, :]), 0.0)
            acts[0, e, p] = (positive * positive).astype(bf16)
            grad = nt_dot(got[1], wout[e, part, :])
            acts[1, e, p] = (grad * 2.0 * positive).astype(bf16)
        for k, weight in ((0, wout), (1, win)):
            act = jnp.concatenate([acts[k, e, p] for p in range(pieces)], axis=1)
            for h in range(heads):
                out = nn_dot(act, weight[e, :, h * width:(h + 1) * width])
                yown[h, :, k, e] = out.astype(bf16).reshape(chunks, rows, width)
        return carry

    lax.fori_loop(0, local, expert, 0)

    def share(d, c):
        return remote(
            yown.at[head_at[d], c], yland.at[d - 1, c], os_.at[d - 1, c], or_.at[d - 1, c],
            {"head": head_at[d]},
        )

    def share_start(k, carry):
        for d in range(1, heads):
            share(d, chunks - 1 - k).start()
        return carry

    lax.fori_loop(0, chunks, share_start, 0)

    def weight_grads(e, carry):
        for p in range(pieces):
            for h in range(heads):
                for w in range(2):
                    piece = tn_dot(acts[1 - w, e, p], taken(w, e, h)).astype(bf16)
                    for s in range(width // 128):
                        dest = h * (width // 128) + s
                        parts[dest % 2, dest // 2, w, e, p * 256:(p + 1) * 256, :] = (
                            piece[:, s * 128:(s + 1) * 128]
                        )
        return carry

    lax.fori_loop(0, local, weight_grads, 0)
    pair_copy = remote(parts.at[1 - core], pair, ps.at[0], pr.at[0], sibling)
    pair_copy.start()

    def combine(c):
        for d in range(1, heads):
            share(d, c).wait_recv()
        total = yown[head, c].astype(f32)
        for d in range(1, heads):
            total = total + yland[d - 1, c].astype(f32)
        out = total[0].reshape(local * rows, width) * gates[c][:, :1]
        back = total[1].reshape(local * rows, width)
        total = jnp.concatenate([out, back], axis=0).astype(bf16)
        for q in range(GROUP):
            contrib[c * GROUP + q] = tn_dot(picks[c * GROUP + q], total)[:both].astype(bf16)

    def target_right(j):
        return 2 * (half - j) - jnp.where(j == 0, 1, 0)

    def target_left(j):
        return 2 * (half - 1 - j) - 1

    def sum_right(j):
        return remote(
            contrib.at[target_right(j)], from_left.at[j], rs.at[0, j], rr.at[0, j], to_right
        )

    def sum_left(j):
        return remote(
            contrib.at[target_left(j)], from_right.at[j], rs.at[1, j], rr.at[1, j], to_left
        )

    def cross_copy(d):
        return remote(
            parts.at[core, x_at[d]], cross.at[d - 1], cs.at[d - 1], cr.at[d - 1],
            {"dp": x_at[d] * 2 + core},
        )

    combine(chunks - 1)

    def add(a, b):
        return (a.astype(f32) + b.astype(f32)).astype(bf16)

    def sum_step(j, carry):
        @pl.when(j > 0)
        def _():
            sum_right(j - 1).wait_recv()
            to = target_right(j)
            contrib[to] = add(contrib[to], from_left[j - 1])

        sum_right(j).start()

        @pl.when((j > 0) & (j < half - 1))
        def _():
            sum_left(j - 1).wait_recv()
            to = target_left(j)
            contrib[to] = add(contrib[to], from_right[j - 1])

        @pl.when(j < half - 1)
        def _():
            sum_left(j).start()

        @pl.when((lax.rem(j, 4) == 2) & (j < half - 4))
        def _():
            combine(chunks - 2 - j // 4)

        @pl.when(j == 1)
        def _():
            pair_copy.wait()

            def merge(k, inner):
                x, w, e = k // (2 * local), (k // local) % 2, k % local
                parts[core, x, w, e] = add(parts[core, x, w, e], pair[x, w, e])
                return inner

            lax.fori_loop(0, xs * 2 * local, merge, 0)
            for d in range(1, xs):
                cross_copy(d).start()

        return carry

    lax.fori_loop(0, half, sum_step, 0)
    sum_right(half - 1).wait_recv()
    sum_left(half - 2).wait_recv()
    mine = contrib[0].astype(f32) + from_left[half - 1].astype(f32)
    mine = (mine + from_right[half - 2].astype(f32)).astype(bf16)
    columns = pl.ds(pl.multiple_of(head * width, width), width)
    tok_ref[:, columns] = mine

    def tell(d):
        return remote(
            tok_ref.at[:, columns], tok_ref.at[:, columns], ts.at[d - 1], tr.at[d - 1],
            {"head": head_at[d]},
        )

    for d in range(1, heads):
        tell(d).start()
    for d in range(1, xs):
        cross_copy(d).wait()

    def finish(k, carry):
        w, e = k // local, k % local
        total = parts[core, px, w, e].astype(f32)
        for d in range(1, xs):
            total = total + cross[d - 1, w, e].astype(f32)
        wgrad_ref[w, e] = total.astype(bf16)
        return carry

    lax.fori_loop(0, 2 * local, finish, 0)

    def drain_ring(i, carry):
        ring_right(i).wait_send()
        sum_right(i - 1).wait_send()

        @pl.when(i < half)
        def _():
            ring_left(i).wait_send()
            sum_left(i - 1).wait_send()

        return carry

    lax.fori_loop(1, half + 1, drain_ring, 0)

    def drain_share(c, carry):
        for d in range(1, heads):
            share(d, c).wait_send()
        return carry

    lax.fori_loop(0, chunks, drain_share, 0)
    for d in range(1, heads):
        tell(d).wait()


def on_device(latent, cotangent, routes, gate_values, weight_in, weight_out):
    tokens, latent_width = latent.shape
    owners = lax.axis_size("expert")
    heads = lax.axis_size("head")
    xs = lax.axis_size("dp") // 2
    local, hidden, _ = weight_in.shape
    width = latent_width // heads
    head = lax.axis_index("head")
    both = 2 * tokens
    half = owners // 2
    chunks = owners // GROUP
    rows = GROUP * CAPACITY

    data = jnp.concatenate([latent, cotangent], 0)
    data = lax.dynamic_slice(data, (0, head * width), (both, width))
    named = routes.T.astype(f32)
    gate = gate_values.T
    high = lax.reduce_precision(gate, 8, 7)
    middle = lax.reduce_precision(gate - high, 8, 7)
    low = lax.reduce_precision(gate - high - middle, 8, 7)

    def on_grads(piece):
        return jnp.pad(piece, ((0, 0), (tokens, 128 - both)))

    named = jnp.pad(
        jnp.concatenate([named, named], 1), ((0, 0), (0, 128 - both)), constant_values=-1.0
    )
    meta = jnp.concatenate(
        [
            jnp.concatenate([named, on_grads(middle)], 1),
            jnp.concatenate([on_grads(high), on_grads(low)], 1),
        ],
        0,
    )
    block = jnp.concatenate([data, meta.astype(bf16)], 0)

    dma = pltpu.SemaphoreType.DMA
    vmem = pltpu.VMEM
    tokens_out, grads_out = pl.pallas_call(
        functools.partial(kernel, (owners, heads, xs, tokens, local)),
        out_shape=(
            jax.ShapeDtypeStruct((both, latent_width), bf16),
            jax.ShapeDtypeStruct((2, local, hidden, 128), bf16),
        ),
        in_specs=[
            pl.BlockSpec(memory_space=pltpu.VMEM),
            pl.BlockSpec(memory_space=pl.ANY),
            pl.BlockSpec(memory_space=pl.ANY),
        ],
        out_specs=(
            pl.BlockSpec(memory_space=pltpu.VMEM),
            pl.BlockSpec(memory_space=pltpu.VMEM),
        ),
        scratch_shapes=[
            vmem((owners, both + 16, width), bf16),
            vmem((owners, 2 * local * rows, 128), bf16),
            vmem((chunks, local * rows, 128), f32),
            vmem((heads, chunks, 2, local, rows, width), bf16),
            vmem((local, hidden, latent_width), bf16),
            vmem((local, hidden, latent_width), bf16),
            vmem((2, local, hidden // 256, chunks * rows, 256), bf16),
            vmem((heads, chunks, 2, local, rows, width), bf16),
            vmem((heads - 1, chunks, 2, local, rows, width), bf16),
            vmem((owners, both, width), bf16),
            vmem((half, both, width), bf16),
            vmem((half - 1, both, width), bf16),
            vmem((2, xs, 2, local, hidden, 128), bf16),
            vmem((xs, 2, local, hidden, 128), bf16),
            vmem((xs - 1, 2, local, hidden, 128), bf16),
            dma((2,)),
            dma((2, half + 1)),
            dma((2, half + 1)),
            dma((heads - 1, chunks)),
            dma((heads - 1, chunks)),
            dma((heads - 1, chunks)),
            dma((heads - 1, chunks)),
            dma((2, half)),
            dma((2, half)),
            dma((1,)),
            dma((1,)),
            dma((xs - 1,)),
            dma((xs - 1,)),
            dma((heads - 1,)),
            dma((heads - 1,)),
        ],
        compiler_params=pltpu.CompilerParams(
            collective_id=0, has_side_effects=True, vmem_limit_bytes=48 * 1024 * 1024
        ),
        name="experts",
    )(block, weight_in, weight_out)
    return tokens_out[:tokens], tokens_out[tokens:], grads_out[0], grads_out[1]


def solution(mesh):
    in_specs = (
        P(("dp", "expert"), None),
        P(("dp", "expert"), None),
        P(("dp", "expert"), None),
        P(("dp", "expert"), None),
        P("expert", "head", None),
        P("expert", "head", None),
    )
    out_specs = (
        P(("dp", "expert"), None),
        P(("dp", "expert"), None),
        P("expert", "head", "dp"),
        P("expert", "head", "dp"),
    )
    return jax.shard_map(
        on_device, mesh=mesh, in_specs=in_specs, out_specs=out_specs, check_vma=False
    )
```

time: 591 us -> 155 us (0.26)
  waiting for transfers between devices: 436 us -> 0 us
  Pallas kernels: 0 us -> 147 us
  blocking collectives: 81.8 us -> 0 us
  local copies, waits for them, and re-layouts: 32.9 us -> 4.68 us
  between operations: 14.1 us -> 0.65 us
  other arithmetic: 12.1 us -> 2.29 us
  matrix products: 9.3 us -> 0 us
    unnamed x7 -> x0, waiting for transfers between devices: 275 us -> none
    pallas_call x0 -> x1, Pallas kernels: none -> 147 us  [on_device(): pl.pallas_call(functools.partial(kernel, (owners, heads, xs, tokens, loca...]
    all_gather x2 -> x0, waiting for transfers between devices: 115 us -> none  [the longest x1 71.9 us: on_device(): data = lax.all_gather(own, 'expert', axis=0)]
    all_gather x2 -> x0, blocking collectives: 81.8 us -> none  [the longest x1 69.4 us: on_device(): meta = lax.all_gather(meta, 'expert', axis=0)]
    reduce_scatter x1 -> x0, waiting for transfers between devices: 44.9 us -> none  [on_device(): share = lax.psum_scatter(parts, 'head', scatter_dimension=3, tiled=True)]
    unnamed x17 -> x4, local copies, waits for them, and re-layouts: 24.9 us -> 3.18 us
    dot_general x10 -> x0, matrix products: 9.3 us -> none  [the longest x1 1.98 us: on_device(): jnp.einsum('ech,ecl->ehl', grad_pre, got_rows, preferred_element_type=f32)]
    another operation x5 -> x2, other arithmetic: 8.53 us -> 1.38 us  [the longest x1 2.89 us: on_device(): rank = jnp.cumsum(count, axis=1) - count]
  transfers between devices with their start and end apart: 5 -> 0, of which waited for: 5 -> 0; matrix products, arithmetic and copies ran while one was open for 6% -> 0% of each run, Pallas kernels for 0% -> 0%
where the time goes in v2:
time: 155 us; the launch traced here: 154 us
  Pallas kernels  147 us (95%)
  local copies, waits for them, and re-layouts  4.68 us (3%)
  other arithmetic  2.29 us (1%)
    pallas_call x1, Pallas kernels, on_device(): pl.pallas_call(functools.partial(kernel, (owners, heads, xs, tokens, loca...  147 us
    unnamed x4, local copies, waits for them, and re-layouts  3.18 us

profile of v2, /device:TPU:6, one launch (start us, length us, event | category | flops | bytes accessed | tf_op | source)
XLA Modules:
  0.0 154.2 jit_solution(6388628645745412930)
XLA Ops:
  0.6 0.7 fusion.19
  1.3 0.1 fusion.20
  1.4 0.7 reduce-precision_convert_fusion
  2.1 0.7 fusion.14
  2.8 0.1 fusion.12.blk_ref
  2.9 0.0 copy-start
  2.9 1.6 %copy-done = bf16[2,512,1024]{2,1,0:T(8,128)(2,1)S(1)} copy-done((bf16[2,512,1024]{2,1,0:T(8,128)(2,1)S(1)}, bf16[2,512,1024]{2,1,0:T(8,128)(2,1)}, u32[]{:S(2)}) %copy-start) | copy-done | bytes 2097176
  4.5 0.0 copy-start.1
  4.5 1.6 %copy-done.1 = bf16[2,512,1024]{2,1,0:T(8,128)(2,1)S(1)} copy-done((bf16[2,512,1024]{2,1,0:T(8,128)(2,1)S(1)}, bf16[2,512,1024]{2,1,0:T(8,128)(2,1)}, u32[]{:S(2)}) %copy-start.1) | copy-done | bytes 2097176
  6.1 146.6 %experts.1 = (bf16[80,1024]{1,0:T(8,128)(2,1)S(1)}, bf16[2,2,512,128]{3,2,1,0:T(8,128)(2,1)S(1)}) custom-call(bf16[96,256]{1,0:T(8,128)(2,1)S(1)} %fusion.12.blk_ref, bf16[2,512,1024]{2,1,0:T(8,128)(2,1)S(1)} %copy-done, bf16[2,512,1024]{2,1,0:T(8,128)(2,1)S(1)} %copy-done.1), custom_call_target="tpu_custom_call" | custom-call | tf_op jit(solution)/shard_map/experts/pallas_call | solution.py:375
  152.7 0.7 fusion.21
  153.4 0.8 slice_bitcast_fusion
Async XLA Ops:
  2.9 1.6 %copy-start = (bf16[2,512,1024]{2,1,0:T(8,128)(2,1)S(1)}, bf16[2,512,1024]{2,1,0:T(8,128)(2,1)}, u32[]{:S(2)}) copy-start(bf16[2,512,1024]{2,1,0:T(8,128)(2,1)} %win_hbm.1) | copy-start | bytes 6291460
  4.5 1.6 %copy-start.1 = (bf16[2,512,1024]{2,1,0:T(8,128)(2,1)S(1)}, bf16[2,512,1024]{2,1,0:T(8,128)(2,1)}, u32[]{:S(2)}) copy-start(bf16[2,512,1024]{2,1,0:T(8,128)(2,1)} %wout_hbm.1) | copy-start | bytes 6291460

commit v3 on v2

--- a/solution.py
+++ b/solution.py
@@ -27,12 +27,13 @@
 
 def kernel(
     dims, blk_ref, win_hbm, wout_hbm, tok_ref, wgrad_ref,
-    ring, picks, gates, xrows, win, wout, acts, yown, yland, contrib, from_left, from_right,
+    ring, picks, gates, xrows, win, wout, acts, yown, yland, contrib, landed,
     parts, pair, cross,
     w_sem, zs, zr, ys, yr, os_, or_, rs, rr, ps, pr, cs, cr, ts, tr,
 ):
     owners, heads, xs, tokens, local = dims
     half = owners // 2
+    hops = half // 2
     chunks = owners // GROUP
     rows = GROUP * CAPACITY
     both = 2 * tokens
@@ -44,8 +45,8 @@
     head = lax.axis_index("head")
     dp = lax.axis_index("dp")
     px, core = dp // 2, dp % 2
-    right, left = lax.rem(me + 1, owners), lax.rem(me + owners - 1, owners)
-    to_right, to_left = {"expert": right}, {"expert": left}
+    ahead = [{"expert": lax.rem(me + d, owners)} for d in (1, 2)]
+    behind = [{"expert": lax.rem(me + owners - d, owners)} for d in (1, 2)]
     head_at = [lax.rem(head + d, heads) for d in range(heads)]
     x_at = [lax.rem(px + d, xs) for d in range(xs)]
     sibling = {"dp": px * 2 + 1 - core}
@@ -63,23 +64,32 @@
     ring[0] = blk_ref[...]
 
     barrier = pltpu.get_barrier_semaphore()
-    partners = [to_right, to_left, sibling]
+    partners = ahead + behind + [sibling]
     partners += [{"head": head_at[d]} for d in range(1, heads)]
     partners += [{"dp": x_at[d] * 2 + core} for d in range(1, xs)]
     for device in partners:
         pl.semaphore_signal(barrier, inc=1, device_id=device, device_id_type=MESH)
     pl.semaphore_wait(barrier, len(partners))
 
-    def slot_right(i):
-        return jnp.maximum(2 * i - 1, 0)
-
-    def ring_right(i):
-        return remote(
-            ring.at[slot_right(i - 1)], ring.at[slot_right(i)], zs.at[0, i], zr.at[0, i], to_right
-        )
-
-    def ring_left(i):
-        return remote(ring.at[2 * (i - 1)], ring.at[2 * i], zs.at[1, i], zr.at[1, i], to_left)
+    def slot_ahead(d):
+        return jnp.maximum(2 * d - 1, 0)
+
+    def piece_of(s, total):
+        return pl.ds(0, 48) if s == 0 else pl.ds(48, total - 48)
+
+    def go_ahead(k, side, s):
+        to, part = 2 * k - side, piece_of(s, both + 16)
+        return remote(
+            ring.at[slot_ahead(2 * k - 2), part], ring.at[slot_ahead(to), part],
+            zs.at[0, to, s], zr.at[0, to, s], ahead[1 - side],
+        )
+
+    def go_behind(k, side, s):
+        to, part = 2 * k - side, piece_of(s, both + 16)
+        return remote(
+            ring.at[2 * (2 * k - 2), part], ring.at[2 * to, part],
+            zs.at[1, to, s], zr.at[1, to, s], behind[1 - side],
+        )
 
     def spread(d, c):
         return remote(
@@ -87,8 +97,10 @@
             {"head": head_at[d]},
         )
 
-    ring_right(1).start()
-    ring_left(1).start()
+    for side in (0, 1):
+        for s in (0, 1):
+            go_ahead(1, side, s).start()
+            go_behind(1, side, s).start()
 
     lane = lax.broadcasted_iota(jnp.int32, (128, 128), 1)
     depth = lax.broadcasted_iota(jnp.int32, (128, 128), 0)
@@ -127,19 +139,30 @@
         xrows[head, c, 1] = (total[local * rows:] * scale).astype(bf16).reshape(local, rows, width)
 
     def gather_group(c, carry):
-        for k in range(4):
-            i = c * 4 + 1 + k
-            ring_right(i).wait_recv()
-
-            @pl.when(i < half)
+        for n in (1, 2):
+            k = 2 * c + n
+            for s in (0, 1):
+                go_ahead(k, 0, s).wait_recv()
+
+                @pl.when(k < hops)
+                def _():
+                    go_ahead(k + 1, 0, s).start()
+                    go_behind(k, 0, s).wait_recv()
+
+                @pl.when(k < hops - 1)
+                def _():
+                    go_behind(k + 1, 0, s).start()
+
+            @pl.when(k < hops)
             def _():
-                ring_right(i + 1).start()
-                ring_left(i).wait_recv()
-
-            @pl.when(i < half - 1)
-            def _():
-                ring_left(i + 1).start()
-
+                for s in (0, 1):
+                    go_ahead(k + 1, 1, s).start()
+                    go_behind(k + 1, 1, s).start()
+
+        for n in (1, 2):
+            for s in (0, 1):
+                go_ahead(2 * c + n, 1, s).wait_recv()
+                go_behind(2 * c + n, 1, s).wait_recv()
         select(c)
         for d in range(1, heads):
             spread(d, c).start()
@@ -217,20 +240,16 @@
         for q in range(GROUP):
             contrib[c * GROUP + q] = tn_dot(picks[c * GROUP + q], total)[:both].astype(bf16)
 
-    def target_right(j):
-        return 2 * (half - j) - jnp.where(j == 0, 1, 0)
-
-    def target_left(j):
-        return 2 * (half - 1 - j) - 1
-
-    def sum_right(j):
-        return remote(
-            contrib.at[target_right(j)], from_left.at[j], rs.at[0, j], rr.at[0, j], to_right
-        )
-
-    def sum_left(j):
-        return remote(
-            contrib.at[target_left(j)], from_right.at[j], rs.at[1, j], rr.at[1, j], to_left
+    def block_ahead(d):
+        return 2 * d - jnp.where(d == half, 1, 0)
+
+    def sum_copy(way, j, s):
+        side, part = way % 2, piece_of(s, both)
+        d = half - side - 2 * j
+        block = block_ahead(d) if way < 2 else 2 * d - 1
+        return remote(
+            contrib.at[block, part], landed.at[way, j, part], rs.at[way, j, s], rr.at[way, j, s],
+            (ahead if way < 2 else behind)[1 - side],
         )
 
     def cross_copy(d):
@@ -239,41 +258,52 @@
             {"dp": x_at[d] * 2 + core},
         )
 
-    combine(chunks - 1)
-
-    def add(a, b):
-        return (a.astype(f32) + b.astype(f32)).astype(bf16)
-
-    def sum_step(j, carry):
-        @pl.when(j > 0)
-        def _():
-            sum_right(j - 1).wait_recv()
-            to = target_right(j)
-            contrib[to] = add(contrib[to], from_left[j - 1])
-
-        sum_right(j).start()
-
-        @pl.when((j > 0) & (j < half - 1))
-        def _():
-            sum_left(j - 1).wait_recv()
-            to = target_left(j)
-            contrib[to] = add(contrib[to], from_right[j - 1])
-
-        @pl.when(j < half - 1)
-        def _():
-            sum_left(j).start()
-
-        @pl.when((lax.rem(j, 4) == 2) & (j < half - 4))
-        def _():
-            combine(chunks - 2 - j // 4)
-
-        @pl.when(j == 1)
+    def sum_into(block, ways, j, s):
+        part = piece_of(s, both)
+        total = contrib[block, part].astype(f32)
+        for way in ways:
+            sum_copy(way, j, s).wait_recv()
+            total = total + landed[way, j, part].astype(f32)
+        contrib[block, part] = total.astype(bf16)
+
+    def sum_group(g, carry):
+        combine(chunks - 1 - g)
+        for n in (0, 1):
+            for s in (0, 1):
+                sum_copy(1, 2 * g + n, s).start()
+                sum_copy(3, 2 * g + n, s).start()
+        for n in (0, 1):
+            j = 2 * g + n
+            d = half - 2 * j
+            for s in (0, 1):
+
+                @pl.when(j > 0)
+                def _():
+                    sum_into(block_ahead(d), (0, 1), j - 1, s)
+
+                sum_copy(0, j, s).start()
+
+                @pl.when(j == 1)
+                def _():
+                    sum_into(2 * d - 1, (3,), j - 1, s)
+
+                @pl.when(j > 1)
+                def _():
+                    sum_into(2 * d - 1, (2, 3), j - 1, s)
+
+                @pl.when(j > 0)
+                def _():
+                    sum_copy(2, j, s).start()
+
+        @pl.when(g == 0)
         def _():
             pair_copy.wait()
 
             def merge(k, inner):
                 x, w, e = k // (2 * local), (k // local) % 2, k % local
-                parts[core, x, w, e] = add(parts[core, x, w, e], pair[x, w, e])
+                parts[core, x, w, e] = (
+                    parts[core, x, w, e].astype(f32) + pair[x, w, e].astype(f32)
+                ).astype(bf16)
                 return inner
 
             lax.fori_loop(0, xs * 2 * local, merge, 0)
@@ -282,11 +312,13 @@
 
         return carry
 
-    lax.fori_loop(0, half, sum_step, 0)
-    sum_right(half - 1).wait_recv()
-    sum_left(half - 2).wait_recv()
-    mine = contrib[0].astype(f32) + from_left[half - 1].astype(f32)
-    mine = (mine + from_right[half - 2].astype(f32)).astype(bf16)
+    lax.fori_loop(0, chunks, sum_group, 0)
+    mine = contrib[0].astype(f32)
+    for way in range(4):
+        for s in (0, 1):
+            sum_copy(way, hops - 1, s).wait_recv()
+        mine = mine + landed[way, hops - 1].astype(f32)
+    mine = mine.astype(bf16)
     columns = pl.ds(pl.multiple_of(head * width, width), width)
     tok_ref[:, columns] = mine
 
@@ -311,18 +343,22 @@
 
     lax.fori_loop(0, 2 * local, finish, 0)
 
-    def drain_ring(i, carry):
-        ring_right(i).wait_send()
-        sum_right(i - 1).wait_send()
-
-        @pl.when(i < half)
-        def _():
-            ring_left(i).wait_send()
-            sum_left(i - 1).wait_send()
-
-        return carry
-
-    lax.fori_loop(1, half + 1, drain_ring, 0)
+    def drain_ring(k, carry):
+        for s in (0, 1):
+            for side in (0, 1):
+                go_ahead(k, side, s).wait_send()
+                sum_copy(side, k - 1, s).wait_send()
+            go_behind(k, 1, s).wait_send()
+            sum_copy(3, k - 1, s).wait_send()
+
+            @pl.when(k < hops)
+            def _():
+                go_behind(k, 0, s).wait_send()
+                sum_copy(2, k, s).wait_send()
+
+        return carry
+
+    lax.fori_loop(1, hops + 1, drain_ring, 0)
 
     def drain_share(c, carry):
         for d in range(1, heads):
@@ -380,8 +416,8 @@
         ),
         in_specs=[
             pl.BlockSpec(memory_space=pltpu.VMEM),
-            pl.BlockSpec(memory_space=pl.ANY),
-            pl.BlockSpec(memory_space=pl.ANY),
+            pl.BlockSpec(memory_space=pltpu.HBM),
+            pl.BlockSpec(memory_space=pltpu.HBM),
         ],
         out_specs=(
             pl.BlockSpec(memory_space=pltpu.VMEM),
@@ -398,20 +434,19 @@
             vmem((heads, chunks, 2, local, rows, width), bf16),
             vmem((heads - 1, chunks, 2, local, rows, width), bf16),
             vmem((owners, both, width), bf16),
-            vmem((half, both, width), bf16),
-            vmem((half - 1, both, width), bf16),
+            vmem((4, half // 2, both, width), bf16),
             vmem((2, xs, 2, local, hidden, 128), bf16),
             vmem((xs, 2, local, hidden, 128), bf16),
             vmem((xs - 1, 2, local, hidden, 128), bf16),
             dma((2,)),
-            dma((2, half + 1)),
-            dma((2, half + 1)),
+            dma((2, half + 1, 2)),
+            dma((2, half + 1, 2)),
             dma((heads - 1, chunks)),
             dma((heads - 1, chunks)),
             dma((heads - 1, chunks)),
             dma((heads - 1, chunks)),
-            dma((2, half)),
-            dma((2, half)),
+            dma((4, half // 2, 2)),
+            dma((4, half // 2, 2)),
             dma((1,)),
             dma((1,)),
             dma((xs - 1,)),
@@ -420,7 +455,7 @@
             dma((heads - 1,)),
         ],
         compiler_params=pltpu.CompilerParams(
-            collective_id=0, has_side_effects=True, vmem_limit_bytes=48 * 1024 * 1024
+            collective_id=0, has_side_effects=True, vmem_limit_bytes=52 * 1024 * 1024
         ),
         name="experts",
     )(block, weight_in, weight_out)

time: 155 us -> 115 us (0.74)
  Pallas kernels: 147 us -> 111 us
  local copies, waits for them, and re-layouts: 4.68 us -> 1.5 us
    pallas_call x1, Pallas kernels: 147 us -> 111 us  [on_device(): pl.pallas_call(functools.partial(kernel, (owners, heads, xs, tokens, loca...]
    unnamed x4 -> x0, local copies, waits for them, and re-layouts: 3.18 us -> none
where the time goes in v3:
time: 115 us
  Pallas kernels  111 us (97%)
  other arithmetic  2.29 us (2%)
  local copies, waits for them, and re-layouts  1.5 us (1%)
    pallas_call x1, Pallas kernels, on_device(): pl.pallas_call(functools.partial(kernel, (owners, heads, xs, tokens, loca...  111 us

profile of v3, /device:TPU:6, one launch (start us, length us, event | category | flops | bytes accessed | tf_op | source)
XLA Modules:
  0.0 115.0 jit_solution(1466579917026797906)
XLA Ops:
  0.6 0.7 fusion.19
  1.3 0.1 fusion.20
  1.4 0.7 reduce-precision_convert_fusion
  2.1 0.7 fusion.14
  2.8 0.1 fusion.12.blk_ref
  2.9 110.5 %experts.1 = (bf16[80,1024]{1,0:T(8,128)(2,1)S(1)}, bf16[2,2,512,128]{3,2,1,0:T(8,128)(2,1)S(1)}) custom-call(bf16[96,256]{1,0:T(8,128)(2,1)S(1)} %fusion.12.blk_ref, bf16[2,512,1024]{2,1,0:T(8,128)(2,1)} %win_hbm.1, bf16[2,512,1024]{2,1,0:T(8,128)(2,1)} %wout_hbm.1), custom_call_target="tpu_custom_call" | custom-call | tf_op jit(solution)/shard_map/experts/pallas_call | solution.py:411
  113.4 0.7 fusion.21
  114.1 0.8 slice_bitcast_fusion

commit v4 on v3

--- a/solution.py
+++ b/solution.py
@@ -26,8 +26,8 @@
 
 
 def kernel(
-    dims, blk_ref, win_hbm, wout_hbm, tok_ref, wgrad_ref,
-    ring, picks, gates, xrows, win, wout, acts, yown, yland, contrib, landed,
+    dims, latent_hbm, cotangent_hbm, routes_hbm, gate_hbm, win_hbm, wout_hbm,
+    moe_ref, back_ref, in_grad_hbm, out_grad_hbm, tok_ref, latent_ref, cotangent_ref, routes_ref, gate_ref, wgrad_ref, ring, picks, gates, xrows, win, wout, acts, yown, yland, contrib, landed,
     parts, pair, cross,
     w_sem, zs, zr, ys, yr, os_, or_, rs, rr, ps, pr, cs, cr, ts, tr,
 ):
@@ -57,11 +57,21 @@
             device_id=device, device_id_type=MESH,
         )
 
+    small = [
+        pltpu.make_async_copy(src, dst, w_sem.at[2 + i])
+        for i, (src, dst) in enumerate(
+            [
+                (latent_hbm, latent_ref),
+                (cotangent_hbm, cotangent_ref),
+                (routes_hbm, routes_ref),
+                (gate_hbm, gate_ref),
+            ]
+        )
+    ]
+    for copy in small:
+        copy.start()
     load_in = pltpu.make_async_copy(win_hbm, win, w_sem.at[0])
     load_out = pltpu.make_async_copy(wout_hbm, wout, w_sem.at[1])
-    load_in.start()
-    load_out.start()
-    ring[0] = blk_ref[...]
 
     barrier = pltpu.get_barrier_semaphore()
     partners = ahead + behind + [sibling]
@@ -69,6 +79,33 @@
     partners += [{"dp": x_at[d] * 2 + core} for d in range(1, xs)]
     for device in partners:
         pl.semaphore_signal(barrier, inc=1, device_id=device, device_id_type=MESH)
+
+    load_in.start()
+    load_out.start()
+    for copy in small:
+        copy.wait()
+    columns = pl.ds(pl.multiple_of(head * width, width), width)
+    own = [latent_ref[:, columns].astype(f32), cotangent_ref[:, columns].astype(f32)]
+    ring[0, :both] = jnp.concatenate(own, axis=0).astype(bf16)
+    token_id = lax.broadcasted_iota(jnp.int32, (tokens, 128), 0)
+    lane_id = lax.broadcasted_iota(jnp.int32, (tokens, 128), 1)
+    on_grads = lane_id == token_id + tokens
+    on_rows = lane_id == token_id
+    spare = lax.broadcasted_iota(jnp.int32, (8, 128), 1) >= both
+    twice = jnp.where(on_rows | on_grads, 1.0, 0.0).astype(bf16)
+    once = jnp.where(on_grads, 1.0, 0.0).astype(bf16)
+    named = nn_dot(routes_ref[...].astype(f32).astype(bf16), twice)
+    named = jnp.where(spare, -1.0, named)
+    rest = gate_ref[...]
+    pieces_of_gate = []
+    for _ in range(3):
+        piece = rest.astype(bf16)
+        pieces_of_gate.append(nn_dot(piece, once))
+        rest = rest - piece.astype(f32)
+    high, middle, low = pieces_of_gate
+    top = jnp.concatenate([named, middle], axis=1)
+    bottom = jnp.concatenate([high, low], axis=1)
+    ring[0, both:] = jnp.concatenate([top, bottom], axis=0).astype(bf16)
     pl.semaphore_wait(barrier, len(partners))
 
     def slot_ahead(d):
@@ -182,6 +219,12 @@
     def taken(kind, e, h):
         return xrows[h, :, kind, e].reshape(chunks * rows, width)
 
+    def share(d, c, e):
+        return remote(
+            yown.at[head_at[d], c, e], yland.at[d - 1, c, e],
+            os_.at[d - 1, c, e], or_.at[d - 1, c, e], {"head": head_at[d]},
+        )
+
     def expert(e, carry):
         got = [jnp.concatenate([taken(k, e, h) for h in range(heads)], axis=1) for k in range(2)]
         for p in range(pieces):
@@ -194,23 +237,20 @@
             act = jnp.concatenate([acts[k, e, p] for p in range(pieces)], axis=1)
             for h in range(heads):
                 out = nn_dot(act, weight[e, :, h * width:(h + 1) * width])
-                yown[h, :, k, e] = out.astype(bf16).reshape(chunks, rows, width)
+                yown[h, :, e, k] = out.astype(bf16).reshape(chunks, rows, width)
+        for d in range(1, heads):
+            share(d, chunks - 1, e).start()
         return carry
 
     lax.fori_loop(0, local, expert, 0)
 
-    def share(d, c):
-        return remote(
-            yown.at[head_at[d], c], yland.at[d - 1, c], os_.at[d - 1, c], or_.at[d - 1, c],
-            {"head": head_at[d]},
-        )
-
     def share_start(k, carry):
-        for d in range(1, heads):
-            share(d, chunks - 1 - k).start()
-        return carry
-
-    lax.fori_loop(0, chunks, share_start, 0)
+        for e in range(local):
+            for d in range(1, heads):
+                share(d, chunks - 1 - k, e).start()
+        return carry
+
+    lax.fori_loop(1, chunks, share_start, 0)
 
     def weight_grads(e, carry):
         for p in range(pieces):
@@ -230,13 +270,15 @@
 
     def combine(c):
         for d in range(1, heads):
-            share(d, c).wait_recv()
+            for e in range(local):
+                share(d, c, e).wait_recv()
         total = yown[head, c].astype(f32)
         for d in range(1, heads):
             total = total + yland[d - 1, c].astype(f32)
-        out = total[0].reshape(local * rows, width) * gates[c][:, :1]
-        back = total[1].reshape(local * rows, width)
-        total = jnp.concatenate([out, back], axis=0).astype(bf16)
+        scale = gates[c][:, :1]
+        out = [total[e, 0] * scale[e * rows:(e + 1) * rows] for e in range(local)]
+        back = [total[e, 1] for e in range(local)]
+        total = jnp.concatenate(out + back, axis=0).astype(bf16)
         for q in range(GROUP):
             contrib[c * GROUP + q] = tn_dot(picks[c * GROUP + q], total)[:both].astype(bf16)
 
@@ -319,7 +361,6 @@
             sum_copy(way, hops - 1, s).wait_recv()
         mine = mine + landed[way, hops - 1].astype(f32)
     mine = mine.astype(bf16)
-    columns = pl.ds(pl.multiple_of(head * width, width), width)
     tok_ref[:, columns] = mine
 
     def tell(d):
@@ -342,6 +383,12 @@
         return carry
 
     lax.fori_loop(0, 2 * local, finish, 0)
+    stores = [
+        pltpu.make_async_copy(wgrad_ref.at[0], in_grad_hbm, w_sem.at[6]),
+        pltpu.make_async_copy(wgrad_ref.at[1], out_grad_hbm, w_sem.at[7]),
+    ]
+    for copy in stores:
+        copy.start()
 
     def drain_ring(k, carry):
         for s in (0, 1):
@@ -362,12 +409,18 @@
 
     def drain_share(c, carry):
         for d in range(1, heads):
-            share(d, c).wait_send()
+            for e in range(local):
+                share(d, c, e).wait_send()
         return carry
 
     lax.fori_loop(0, chunks, drain_share, 0)
     for d in range(1, heads):
         tell(d).wait()
+    whole = tok_ref[...].astype(f32)
+    moe_ref[...] = whole[:tokens].astype(bf16)
+    back_ref[...] = whole[tokens:].astype(bf16)
+    for copy in stores:
+        copy.wait()
 
 
 def on_device(latent, cotangent, routes, gate_values, weight_in, weight_out):
@@ -377,53 +430,42 @@
     xs = lax.axis_size("dp") // 2
     local, hidden, _ = weight_in.shape
     width = latent_width // heads
-    head = lax.axis_index("head")
     both = 2 * tokens
     half = owners // 2
     chunks = owners // GROUP
     rows = GROUP * CAPACITY
 
-    data = jnp.concatenate([latent, cotangent], 0)
-    data = lax.dynamic_slice(data, (0, head * width), (both, width))
-    named = routes.T.astype(f32)
-    gate = gate_values.T
-    high = lax.reduce_precision(gate, 8, 7)
-    middle = lax.reduce_precision(gate - high, 8, 7)
-    low = lax.reduce_precision(gate - high - middle, 8, 7)
-
-    def on_grads(piece):
-        return jnp.pad(piece, ((0, 0), (tokens, 128 - both)))
-
-    named = jnp.pad(
-        jnp.concatenate([named, named], 1), ((0, 0), (0, 128 - both)), constant_values=-1.0
-    )
-    meta = jnp.concatenate(
-        [
-            jnp.concatenate([named, on_grads(middle)], 1),
-            jnp.concatenate([on_grads(high), on_grads(low)], 1),
-        ],
-        0,
-    )
-    block = jnp.concatenate([data, meta.astype(bf16)], 0)
-
     dma = pltpu.SemaphoreType.DMA
     vmem = pltpu.VMEM
-    tokens_out, grads_out = pl.pallas_call(
+    return pl.pallas_call(
         functools.partial(kernel, (owners, heads, xs, tokens, local)),
         out_shape=(
-            jax.ShapeDtypeStruct((both, latent_width), bf16),
-            jax.ShapeDtypeStruct((2, local, hidden, 128), bf16),
+            jax.ShapeDtypeStruct((tokens, latent_width), bf16),
+            jax.ShapeDtypeStruct((tokens, latent_width), bf16),
+            jax.ShapeDtypeStruct((local, hidden, 128), bf16),
+            jax.ShapeDtypeStruct((local, hidden, 128), bf16),
         ),
         in_specs=[
-            pl.BlockSpec(memory_space=pltpu.VMEM),
+            pl.BlockSpec(memory_space=pltpu.HBM),
+            pl.BlockSpec(memory_space=pltpu.HBM),
+            pl.BlockSpec(memory_space=pltpu.HBM),
+            pl.BlockSpec(memory_space=pltpu.HBM),
             pl.BlockSpec(memory_space=pltpu.HBM),
             pl.BlockSpec(memory_space=pltpu.HBM),
         ],
         out_specs=(
             pl.BlockSpec(memory_space=pltpu.VMEM),
             pl.BlockSpec(memory_space=pltpu.VMEM),
+            pl.BlockSpec(memory_space=pltpu.HBM),
+            pl.BlockSpec(memory_space=pltpu.HBM),
         ),
         scratch_shapes=[
+            vmem((both, latent_width), bf16),
+            vmem((tokens, latent_width), bf16),
+            vmem((tokens, latent_width), bf16),
+            vmem(routes.T.shape, jnp.int32),
+            vmem(routes.T.shape, f32),
+            vmem((2, local, hidden, 128), bf16),
             vmem((owners, both + 16, width), bf16),
             vmem((owners, 2 * local * rows, 128), bf16),
             vmem((chunks, local * rows, 128), f32),
@@ -431,20 +473,20 @@
             vmem((local, hidden, latent_width), bf16),
             vmem((local, hidden, latent_width), bf16),
             vmem((2, local, hidden // 256, chunks * rows, 256), bf16),
-            vmem((heads, chunks, 2, local, rows, width), bf16),
-            vmem((heads - 1, chunks, 2, local, rows, width), bf16),
+            vmem((heads, chunks, local, 2, rows, width), bf16),
+            vmem((heads - 1, chunks, local, 2, rows, width), bf16),
             vmem((owners, both, width), bf16),
             vmem((4, half // 2, both, width), bf16),
             vmem((2, xs, 2, local, hidden, 128), bf16),
             vmem((xs, 2, local, hidden, 128), bf16),
             vmem((xs - 1, 2, local, hidden, 128), bf16),
-            dma((2,)),
+            dma((8,)),
             dma((2, half + 1, 2)),
             dma((2, half + 1, 2)),
             dma((heads - 1, chunks)),
             dma((heads - 1, chunks)),
-            dma((heads - 1, chunks)),
-            dma((heads - 1, chunks)),
+            dma((heads - 1, chunks, local)),
+            dma((heads - 1, chunks, local)),
             dma((4, half // 2, 2)),
             dma((4, half // 2, 2)),
             dma((1,)),
@@ -455,11 +497,10 @@
             dma((heads - 1,)),
         ],
         compiler_params=pltpu.CompilerParams(
-            collective_id=0, has_side_effects=True, vmem_limit_bytes=52 * 1024 * 1024
+            collective_id=0, has_side_effects=True, vmem_limit_bytes=60 * 1024 * 1024
         ),
         name="experts",
-    )(block, weight_in, weight_out)
-    return tokens_out[:tokens], tokens_out[tokens:], grads_out[0], grads_out[1]
+    )(latent, cotangent, routes.T, gate_values.T, weight_in, weight_out)
 
 
 def solution(mesh):

time: 115 us -> 119 us (1.035)
  local copies, waits for them, and re-layouts: 1.5 us -> 6.39 us
  other arithmetic: 2.29 us -> 0 us
    unnamed x0 -> x4, local copies, waits for them, and re-layouts: none -> 6.39 us
    another operation x2 -> x0, other arithmetic: 1.38 us -> none
    pallas_call x1, Pallas kernels: 111 us -> 112 us  [on_device(): pl.pallas_call(functools.partial(kernel, (owners, heads, xs, tokens, loca...]
where the time goes in v4:
time: 119 us
  Pallas kernels  112 us (94%)
  local copies, waits for them, and re-layouts  6.39 us (5%)
    pallas_call x1, Pallas kernels, on_device(): pl.pallas_call(functools.partial(kernel, (owners, heads, xs, tokens, loca...  112 us
    unnamed x4, local copies, waits for them, and re-layouts  6.39 us

profile of v4, /device:TPU:6, one launch (start us, length us, event | category | flops | bytes accessed | tf_op | source)
XLA Modules:
  0.0 118.9 jit_solution(16787109127364054456)
XLA Ops:
  0.6 111.8 %experts.1 = (bf16[40,1024]{1,0:T(8,128)(2,1)}, bf16[40,1024]{1,0:T(8,128)(2,1)}, bf16[2,512,128]{2,1,0:T(8,128)(2,1)}, bf16[2,512,128]{2,1,0:T(8,128)(2,1)}) custom-call(bf16[40,1024]{1,0:T(8,128)(2,1)} %latent_hbm.1, bf16[40,1024]{1,0:T(8,128)(2,1)} %cotangent_hbm.1, s32[8,40]{1,0:T(8,128)} %bitcast.2, f32[8,40]{1,0:T(8,128)} %bitcast.3, ...), custom_call_target="tpu_custom_call" | custom-call | tf_op jit(solution)/shard_map/experts/pallas_call | solution.py:440
  112.5 1.5 %copy.14 = bf16[40,1024]{1,0:T(8,128)(2,1)} copy(bf16[40,1024]{1,0:T(8,128)(2,1)} %get-tuple-element.8) | data formatting | bytes 163840
  114.0 1.5 %copy.15 = bf16[40,1024]{1,0:T(8,128)(2,1)} copy(bf16[40,1024]{1,0:T(8,128)(2,1)} %get-tuple-element.9) | data formatting | bytes 163840
  115.5 1.7 %copy.16 = bf16[2,512,128]{2,1,0:T(8,128)(2,1)} copy(bf16[2,512,128]{2,1,0:T(8,128)(2,1)} %get-tuple-element.10) | data formatting | bytes 524288
  117.2 1.7 %copy.17 = bf16[2,512,128]{2,1,0:T(8,128)(2,1)} copy(bf16[2,512,128]{2,1,0:T(8,128)(2,1)} %get-tuple-element.11) | data formatting | bytes 524288

commit v5 on v3

--- a/solution.py
+++ b/solution.py
@@ -182,6 +182,12 @@
     def taken(kind, e, h):
         return xrows[h, :, kind, e].reshape(chunks * rows, width)
 
+    def share(d, c, e):
+        return remote(
+            yown.at[head_at[d], c, e], yland.at[d - 1, c, e],
+            os_.at[d - 1, c, e], or_.at[d - 1, c, e], {"head": head_at[d]},
+        )
+
     def expert(e, carry):
         got = [jnp.concatenate([taken(k, e, h) for h in range(heads)], axis=1) for k in range(2)]
         for p in range(pieces):
@@ -194,23 +200,20 @@
             act = jnp.concatenate([acts[k, e, p] for p in range(pieces)], axis=1)
             for h in range(heads):
                 out = nn_dot(act, weight[e, :, h * width:(h + 1) * width])
-                yown[h, :, k, e] = out.astype(bf16).reshape(chunks, rows, width)
+                yown[h, :, e, k] = out.astype(bf16).reshape(chunks, rows, width)
+        for d in range(1, heads):
+            share(d, chunks - 1, e).start()
         return carry
 
     lax.fori_loop(0, local, expert, 0)
 
-    def share(d, c):
-        return remote(
-            yown.at[head_at[d], c], yland.at[d - 1, c], os_.at[d - 1, c], or_.at[d - 1, c],
-            {"head": head_at[d]},
-        )
-
     def share_start(k, carry):
-        for d in range(1, heads):
-            share(d, chunks - 1 - k).start()
-        return carry
-
-    lax.fori_loop(0, chunks, share_start, 0)
+        for e in range(local):
+            for d in range(1, heads):
+                share(d, chunks - 1 - k, e).start()
+        return carry
+
+    lax.fori_loop(1, chunks, share_start, 0)
 
     def weight_grads(e, carry):
         for p in range(pieces):
@@ -230,13 +233,15 @@
 
     def combine(c):
         for d in range(1, heads):
-            share(d, c).wait_recv()
+            for e in range(local):
+                share(d, c, e).wait_recv()
         total = yown[head, c].astype(f32)
         for d in range(1, heads):
             total = total + yland[d - 1, c].astype(f32)
-        out = total[0].reshape(local * rows, width) * gates[c][:, :1]
-        back = total[1].reshape(local * rows, width)
-        total = jnp.concatenate([out, back], axis=0).astype(bf16)
+        scale = gates[c][:, :1]
+        out = [total[e, 0] * scale[e * rows:(e + 1) * rows] for e in range(local)]
+        back = [total[e, 1] for e in range(local)]
+        total = jnp.concatenate(out + back, axis=0).astype(bf16)
         for q in range(GROUP):
             contrib[c * GROUP + q] = tn_dot(picks[c * GROUP + q], total)[:both].astype(bf16)
 
@@ -362,7 +367,8 @@
 
     def drain_share(c, carry):
         for d in range(1, heads):
-            share(d, c).wait_send()
+            for e in range(local):
+                share(d, c, e).wait_send()
         return carry
 
     lax.fori_loop(0, chunks, drain_share, 0)
@@ -431,8 +437,8 @@
             vmem((local, hidden, latent_width), bf16),
             vmem((local, hidden, latent_width), bf16),
             vmem((2, local, hidden // 256, chunks * rows, 256), bf16),
-            vmem((heads, chunks, 2, local, rows, width), bf16),
-            vmem((heads - 1, chunks, 2, local, rows, width), bf16),
+            vmem((heads, chunks, local, 2, rows, width), bf16),
+            vmem((heads - 1, chunks, local, 2, rows, width), bf16),
             vmem((owners, both, width), bf16),
             vmem((4, half // 2, both, width), bf16),
             vmem((2, xs, 2, local, hidden, 128), bf16),
@@ -443,8 +449,8 @@
             dma((2, half + 1, 2)),
             dma((heads - 1, chunks)),
             dma((heads - 1, chunks)),
-            dma((heads - 1, chunks)),
-            dma((heads - 1, chunks)),
+            dma((heads - 1, chunks, local)),
+            dma((heads - 1, chunks, local)),
             dma((4, half // 2, 2)),
             dma((4, half // 2, 2)),
             dma((1,)),

time: 115 us -> 116 us (level)
  no operation moved by 1% of the time
where the time goes in v5:
time: 116 us
  Pallas kernels  111 us (96%)
  other arithmetic  2.29 us (2%)
  local copies, waits for them, and re-layouts  1.5 us (1%)
    pallas_call x1, Pallas kernels, on_device(): pl.pallas_call(functools.partial(kernel, (owners, heads, xs, tokens, loca...  111 us

profile of v5, /device:TPU:6, one launch (start us, length us, event | category | flops | bytes accessed | tf_op | source)
XLA Modules:
  0.0 115.8 jit_solution(16727924681121332508)
XLA Ops:
  0.6 0.7 fusion.19
  1.3 0.1 fusion.20
  1.4 0.7 reduce-precision_convert_fusion
  2.1 0.7 fusion.14
  2.8 0.1 fusion.12.blk_ref
  2.9 111.4 %experts.1 = (bf16[80,1024]{1,0:T(8,128)(2,1)S(1)}, bf16[2,2,512,128]{3,2,1,0:T(8,128)(2,1)S(1)}) custom-call(bf16[96,256]{1,0:T(8,128)(2,1)S(1)} %fusion.12.blk_ref, bf16[2,512,1024]{2,1,0:T(8,128)(2,1)} %win_hbm.1, bf16[2,512,1024]{2,1,0:T(8,128)(2,1)} %wout_hbm.1), custom_call_target="tpu_custom_call" | custom-call | tf_op jit(solution)/shard_map/experts/pallas_call | solution.py:417
  114.3 0.7 fusion.21
  115.0 0.8 slice_bitcast_fusion
